TPU v7x, 256 devices: a whole 4x4x8 slice. The times are simulated.
256 devices in a mesh: depth: 32 (over x, y, core), tile: 8 (over z).
Axes of the slice: x: 4, y: 4, z: 8, core: 2. Of those that a mesh axis runs over, the one named last changes fastest.
Arguments:
- fronts: float32 [32, 8, 8, 2, 128, 128], P('depth', 'tile'), may hold values from -6 to 6
- probe_wave: float32 [2, 128, 128], replicated, may hold values from -6 to 6
- object_slices: bfloat16 [64, 2, 3072, 384], P('depth', None, 'tile')
- patch_list: int32 [35, 8, 3, 8], P(None, 'tile'), may hold values from 0 to 256, as said below
- counts: int32 [35, 8], P(None, 'tile'), may hold values from 1 to 8, as said below
Outputs:
- exit_waves: float32 [32, 8, 8, 2, 128, 128], P('depth', 'tile')
Inputs may be any that keep to these rules, and one draw needn't show every extreme that they name: `patch_list`: rows and columns of corners run from 0 to 256, and that end is reached. Among the live probes of one batch of one owner no tile is named more than 1 times; a batch of 8 probes names every tile exactly 1 times. `counts`: some batch of some owner holds 8 probes.
All inputs are finite; a program needn't handle non-finite values.
Results may differ from a plain program's by a relative error of at most 0.0003.
Values may be sent and summed in bfloat16 or wider, within the bound.
A program may use at most 64 MiB of HBM per device.

v0:
```python
import math
import jax
import jax.numpy as jnp
from jax import lax
from jax.sharding import PartitionSpec as P

STEPS = 4
fresnel_rate = 0.3


def from_behind(value, axis, steps):
    count = lax.axis_size(axis)
    leading, last = (max(0, -steps), min(count, count - steps))
    return lax.ppermute(value, axis, [(source, source + steps) for source in range(leading, last)])


def dft_tables(width, inverse):
    index = jnp.arange(width, dtype=jnp.int32)
    angle = 2.0 * math.pi / width * (index[:, None] * index[None, :] % width).astype(jnp.float32)
    cosine = jnp.cos(angle)
    sine = jnp.sin(angle)
    if inverse:
        cosine = cosine / width
        imagine = sine / width
    else:
        imagine = -sine
    return (cosine, cosine + imagine, imagine - cosine)


def plane_dot(plane, table):
    shape = plane.shape
    flat = plane.reshape(-1, shape[-1])
    return jnp.dot(
        flat, table, precision=lax.Precision.HIGHEST, preferred_element_type=jnp.float32
    ).reshape(shape)


def right_multiply(real_part, imag_part, tables):
    cosine, summed, differ = tables
    first = plane_dot(real_part + imag_part, cosine)
    second = plane_dot(real_part, differ)
    third = plane_dot(imag_part, summed)
    return (first - third, first + second)


def transform(real_part, imag_part, tables):
    real_part, imag_part = right_multiply(real_part, imag_part, tables)
    return right_multiply(jnp.swapaxes(real_part, -1, -2), jnp.swapaxes(imag_part, -1, -2), tables)


def fresnel(width):
    index = jnp.arange(width, dtype=jnp.int32)
    freq = jnp.where(index < width // 2, index, index - width).astype(jnp.float32)
    phase = -2.0 * math.pi * fresnel_rate / width * (freq[:, None] ** 2 + freq[None, :] ** 2)
    return (jnp.cos(phase), jnp.sin(phase))


def slab_pass(wavefield, patches):
    width = wavefield.shape[-1]
    forward = dft_tables(width, False)
    backward = dft_tables(width, True)
    kernel_cos, kernel_sin = fresnel(width)
    real_part = wavefield[:, 0]
    imag_part = wavefield[:, 1]
    for layer in range(2):
        trans_real = patches[:, layer, 0].astype(jnp.float32)
        trans_imag = patches[:, layer, 1].astype(jnp.float32)
        real_part, imag_part = (
            real_part * trans_real - imag_part * trans_imag,
            real_part * trans_imag + imag_part * trans_real,
        )
        spec_real, spec_imag = transform(real_part, imag_part, forward)
        spec_real, spec_imag = (
            spec_real * kernel_cos - spec_imag * kernel_sin,
            spec_real * kernel_sin + spec_imag * kernel_cos,
        )
        real_part, imag_part = transform(spec_real, spec_imag, backward)
    return jnp.stack([real_part, imag_part], axis=1)


def rank_within(tile_ids, live):
    slot_index = jnp.arange(tile_ids.shape[0], dtype=jnp.int32)
    same = (
        (tile_ids[:, None] == tile_ids[None, :])
        & live[None, :]
        & (slot_index[None, :] < slot_index[:, None])
    )
    return jnp.sum(same.astype(jnp.int32), axis=1)


def cut_from(source, row_value, column_value, width):
    zero = jnp.zeros((), jnp.int32)
    return lax.dynamic_slice(source, (zero, zero, row_value, column_value), (2, 2, width, width))


def per_device(fronts, probe_wave, object_slices, patch_list, counts):
    depth_count = lax.axis_size("depth")
    tile_count = lax.axis_size("tile")
    depth_index = lax.axis_index("depth")
    tile_index = lax.axis_index("tile")
    slots = fronts.shape[2]
    width = fronts.shape[-1]
    pair = slots // tile_count
    slot_index = jnp.arange(slots, dtype=jnp.int32)
    own_lists = patch_list[:, 0]
    own_counts = counts[:, 0]
    batch_ids = [step + depth_count - 1 - depth_index for step in range(STEPS)]
    step_lists = jnp.stack(
        [lax.dynamic_index_in_dim(own_lists, batch, 0, keepdims=False) for batch in batch_ids]
    )
    step_counts = jnp.stack(
        [lax.dynamic_index_in_dim(own_counts, batch, 0, keepdims=False) for batch in batch_ids]
    )

    def outgoing(all_lists, all_counts):
        tile_ids = all_lists[:, 0]
        live = slot_index[None, :] < all_counts[:, None]
        order = jax.vmap(rank_within)(tile_ids, live)
        target = live & (tile_ids == tile_index)
        choose = (
            target[:, None, :]
            & (order[:, None, :] == jnp.arange(pair, dtype=jnp.int32)[None, :, None])
        ).astype(jnp.int32)
        row_start = jnp.sum(choose * all_lists[:, 1][:, None, :], axis=-1)
        column_start = jnp.sum(choose * all_lists[:, 2][:, None, :], axis=-1)
        valid = jnp.sum(choose, axis=-1) > 0

        def cut_local(row_value, column_value):
            return cut_from(object_slices, row_value, column_value, width)

        cuts = jax.vmap(jax.vmap(cut_local))(row_start, column_start)
        return jnp.where(valid[:, :, None, None, None, None], cuts, jnp.zeros_like(cuts))

    wavefield = fronts[0, 0]
    for step in range(STEPS):
        listing = step_lists[step]
        count = step_counts[step]
        live = (slot_index < count).astype(jnp.float32)[:, None, None, None]
        if step > 0:
            arrived = from_behind(wavefield, "depth", 1)
            wavefield = jnp.where(depth_index == 0, probe_wave[None] * live, arrived)
        else:
            wavefield = wavefield * live
        got_lists, got_counts = (
            lax.all_gather(listing[None], "tile", axis=0, tiled=True),
            lax.all_gather(count[None], "tile", axis=0, tiled=True),
        )
        received = lax.all_to_all(
            outgoing(got_lists, got_counts), "tile", split_axis=0, concat_axis=0, tiled=True
        )
        incoming_tile_ids = listing[0]
        incoming_live = slot_index < count
        incoming_order = rank_within(incoming_tile_ids, incoming_live)
        place = incoming_tile_ids * pair + jnp.minimum(incoming_order, pair - 1)
        flat = received.reshape((tile_count * pair,) + received.shape[2:])
        patches = jnp.take(flat, place, axis=0)
        wavefield = slab_pass(wavefield, patches)
    return wavefield[None, None]


def solution(mesh):
    in_specs = (
        P("depth", "tile", None, None, None, None),
        P(),
        P("depth", None, "tile", None),
        P(None, "tile", None, None),
        P(None, "tile"),
    )
    out_specs = P("depth", "tile", None, None, None, None)
    return jax.shard_map(
        per_device, mesh=mesh, in_specs=in_specs, out_specs=out_specs, check_vma=False
    )
```

profile of v0, /device:TPU:38, one launch (start us, length us, event | category | flops | bytes accessed | tf_op | source)
XLA Modules:
  0.0 397.6 jit_solution(2629929279038056412)
XLA Ops:
  7.9 15.2 %all-reduce.4 = (s32[8]{0:T(128)S(1)}, s32[8]{0:T(128)S(1)}, s32[8]{0:T(128)S(1)}, s32[8]{0:T(128)S(1)}) all-reduce(s32[8]{0:T(128)S(1)} %bitcast_dynamic-update-slice_fusion.4, s32[8]{0:T(128)S(1)} %bitcast_dynamic-update-slice_fusion.5, s32[8]{0:T(128)S(1)} %bitcast_dynamic-update-slice_fusion.6, ...), channel_id=8, replica_groups=mesh['depth'=32,'tile'=8] {'tile'}, use_global_device_ids=true, to_apply=%add.3 | all-reduce | flops 32 | bytes 256 | tf_op jit(solution)/shard_map/all_gather | solution.py:146
  24.5 20.8 %all-gather.7 = s32[8,1,3,8]{3,1,2,0:T(1,128)S(1)} all-gather(s32[1,1,3,8]{3,1,2,0:T(1,128)S(1)} %copy.293), channel_id=9, replica_groups=mesh['depth'=32,'tile'=8] {'tile'}, dimensions={0}, use_global_device_ids=true | all-gather | bytes 864 | tf_op jit(solution)/shard_map/all_gather | solution.py:145
  45.4 20.7 %all-gather.5 = s32[8,1,3,8]{3,1,2,0:T(1,128)S(1)} all-gather(s32[1,1,3,8]{3,1,2,0:T(1,128)S(1)} %copy.292), channel_id=7, replica_groups=mesh['depth'=32,'tile'=8] {'tile'}, dimensions={0}, use_global_device_ids=true | all-gather | bytes 864 | tf_op jit(solution)/shard_map/all_gather | solution.py:145
  66.2 20.7 %all-gather.3 = s32[8,1,3,8]{3,1,2,0:T(1,128)S(1)} all-gather(s32[1,1,3,8]{3,1,2,0:T(1,128)S(1)} %copy.291), channel_id=5, replica_groups=mesh['depth'=32,'tile'=8] {'tile'}, dimensions={0}, use_global_device_ids=true | all-gather | bytes 864 | tf_op jit(solution)/shard_map/all_gather | solution.py:145
  87.0 21.1 %all-gather.1 = s32[8,1,3,8]{3,1,2,0:T(1,128)S(1)} all-gather(s32[1,1,3,8]{3,1,2,0:T(1,128)S(1)} %copy.290), channel_id=3, replica_groups=mesh['depth'=32,'tile'=8] {'tile'}, dimensions={0}, use_global_device_ids=true | all-gather | bytes 864 | tf_op jit(solution)/shard_map/all_gather | solution.py:145
  110.1 24.6 %while.4 = (s32[]{:T(128)}, bf16[2,2,384,384]{3,2,1,0:T(8,128)(2,1)}, s32[8,4]{0,1:T(4,128)S(1)}, bf16[8,2,2,128,128]{4,3,2,1,0:T(8,128)(2,1)S(1)}, s32[]{:T(128)}) while((s32[]{:T(128)}, bf16[2,2,384,384]{3,2,1,0:T(8,128)(2,1)}, s32[8,4]{0,1:T(4,128)S(1)}, bf16[8,2,2,128,128]{4,3,2,1,0:T(8,128)(2,1)S(1)}, s32[]{:T(128)}) %tuple.93), condition=%wide.while_cond, body=%wide.while_body.sunk | while | flops 2 | bytes 262269 | solution.py:93
  135.9 6.2 %all-to-all-start = ((bf16[8,1,2,2,128,128]{5,4,3,2,1,0:T(8,128)(2,1)}), bf16[8,1,2,2,128,128]{5,4,3,2,1,0:T(8,128)(2,1)S(1)}, u32[]{:S(2)}, u32[]{:S(2)}) async-start(bf16[8,1,2,2,128,128]{5,4,3,2,1,0:T(8,128)(2,1)} %bitcast_select_fusion.3), calls=%async_computation | async-start | bytes 2097152 | tf_op jit(solution)/shard_map/all_to_all | solution.py:148
  145.4 24.1 %while.5 = (s32[]{:T(128)}, bf16[2,2,384,384]{3,2,1,0:T(8,128)(2,1)}, s32[8,4]{0,1:T(4,128)S(1)}, bf16[8,2,2,128,128]{4,3,2,1,0:T(8,128)(2,1)S(1)}, s32[]{:T(128)}) while((s32[]{:T(128)}, bf16[2,2,384,384]{3,2,1,0:T(8,128)(2,1)}, s32[8,4]{0,1:T(4,128)S(1)}, bf16[8,2,2,128,128]{4,3,2,1,0:T(8,128)(2,1)S(1)}, s32[]{:T(128)}) %tuple.105), condition=%wide.while_cond.1, body=%wide.while_body.1.sunk | while | flops 2 | bytes 262269 | solution.py:93
  171.6 29.4 %while.6 = (s32[]{:T(128)}, bf16[2,2,384,384]{3,2,1,0:T(8,128)(2,1)}, s32[8,4]{0,1:T(4,128)S(1)}, bf16[8,2,2,128,128]{4,3,2,1,0:T(8,128)(2,1)}, s32[]{:T(128)}) while((s32[]{:T(128)}, bf16[2,2,384,384]{3,2,1,0:T(8,128)(2,1)}, s32[8,4]{0,1:T(4,128)S(1)}, bf16[8,2,2,128,128]{4,3,2,1,0:T(8,128)(2,1)}, s32[]{:T(128)}) %tuple.106), condition=%wide.while_cond.2, body=%wide.while_body.2.sunk | while | flops 2 | bytes 263793 | solution.py:93
  172.2 3.0 bitcast_dynamic-update-slice_fusion.14
  175.9 3.0 bitcast_dynamic-update-slice_fusion.14
  179.6 3.0 bitcast_dynamic-update-slice_fusion.14
  183.3 3.0 bitcast_dynamic-update-slice_fusion.14
  186.9 3.0 bitcast_dynamic-update-slice_fusion.14
  190.6 3.0 bitcast_dynamic-update-slice_fusion.14
  194.3 3.0 bitcast_dynamic-update-slice_fusion.14
  198.0 3.0 bitcast_dynamic-update-slice_fusion.14
  203.8 23.7 %while.7 = (s32[]{:T(128)}, bf16[2,2,384,384]{3,2,1,0:T(8,128)(2,1)}, s32[8,4]{0,1:T(4,128)S(1)}, bf16[8,2,2,128,128]{4,3,2,1,0:T(8,128)(2,1)S(1)}, s32[]{:T(128)}) while((s32[]{:T(128)}, bf16[2,2,384,384]{3,2,1,0:T(8,128)(2,1)}, s32[8,4]{0,1:T(4,128)S(1)}, bf16[8,2,2,128,128]{4,3,2,1,0:T(8,128)(2,1)S(1)}, s32[]{:T(128)}) %tuple.107), condition=%wide.while_cond.3, body=%wide.while_body.3.sunk | while | flops 2 | bytes 262269 | solution.py:93
  227.5 7.4 %all-to-all-start.1 = ((bf16[8,1,2,2,128,128]{5,4,3,2,1,0:T(8,128)(2,1)}), bf16[8,1,2,2,128,128]{5,4,3,2,1,0:T(8,128)(2,1)}, u32[]{:S(2)}, u32[]{:S(2)}) async-start(bf16[8,1,2,2,128,128]{5,4,3,2,1,0:T(8,128)(2,1)} %bitcast_select_fusion.2), calls=%async_computation.1 | async-start | bytes 2097152 | tf_op jit(solution)/shard_map/all_to_all | solution.py:148
  266.0 7.2 %all-to-all-start.2 = ((bf16[8,1,2,2,128,128]{5,4,3,2,1,0:T(8,128)(2,1)}), bf16[8,1,2,2,128,128]{5,4,3,2,1,0:T(8,128)(2,1)S(1)}, u32[]{:S(2)}, u32[]{:S(2)}) async-start(bf16[8,1,2,2,128,128]{5,4,3,2,1,0:T(8,128)(2,1)} %bitcast_select_fusion.1), calls=%async_computation.2 | async-start | bytes 2097152 | tf_op jit(solution)/shard_map/all_to_all | solution.py:148
  275.3 4.0 %collective-permute-done = f32[8,2,128,128]{3,2,0,1:T(8,128)} collective-permute-done((f32[8,2,128,128]{3,2,0,1:T(8,128)S(1)}, f32[8,2,128,128]{3,2,0,1:T(8,128)}, u32[]{:S(2)}, u32[]{:S(2)}) %collective-permute-start) | collective-permute-done | bytes 1048608 | tf_op jit(solution)/shard_map/ppermute | solution.py:14
  310.8 7.2 %all-to-all-start.3 = ((bf16[8,1,2,2,128,128]{5,4,3,2,1,0:T(8,128)(2,1)}), bf16[8,1,2,2,128,128]{5,4,3,2,1,0:T(8,128)(2,1)S(1)}, u32[]{:S(2)}, u32[]{:S(2)}) async-start(bf16[8,1,2,2,128,128]{5,4,3,2,1,0:T(8,128)(2,1)} %bitcast_select_fusion), calls=%async_computation.3 | async-start | bytes 2097152 | tf_op jit(solution)/shard_map/all_to_all | solution.py:148
  318.9 6.5 %collective-permute-done.1 = f32[8,2,128,128]{3,2,0,1:T(8,128)} collective-permute-done((f32[8,2,128,128]{3,2,0,1:T(8,128)}, f32[8,2,128,128]{3,2,0,1:T(8,128)}, u32[]{:S(2)}, u32[]{:S(2)}) %collective-permute-start.1) | collective-permute-done | bytes 1048608 | tf_op jit(solution)/shard_map/ppermute | solution.py:14
  356.6 14.8 %collective-permute-done.2 = f32[8,2,128,128]{3,2,0,1:T(8,128)S(1)} collective-permute-done((f32[8,2,128,128]{3,2,0,1:T(8,128)}, f32[8,2,128,128]{3,2,0,1:T(8,128)S(1)}, u32[]{:S(2)}, u32[]{:S(2)}) %collective-permute-start.2) | collective-permute-done | bytes 1048608 | tf_op jit(solution)/shard_map/ppermute | solution.py:14
  (290 shorter events, 219.7 us)
Async XLA Ops:
  135.9 91.7 %all-to-all-start = ((bf16[8,1,2,2,128,128]{5,4,3,2,1,0:T(8,128)(2,1)}), bf16[8,1,2,2,128,128]{5,4,3,2,1,0:T(8,128)(2,1)S(1)}, u32[]{:S(2)}, u32[]{:S(2)}) async-start(bf16[8,1,2,2,128,128]{5,4,3,2,1,0:T(8,128)(2,1)} %bitcast_select_fusion.3), calls=%async_computation | async-start | bytes 2097152 | tf_op jit(solution)/shard_map/all_to_all | solution.py:148
  227.5 7.4 %copy-start = (bf16[8,2,2,128,128]{4,3,2,1,0:T(8,128)(2,1)}, bf16[8,2,2,128,128]{4,3,2,1,0:T(8,128)(2,1)S(1)}, u32[]{:S(2)}) copy-start(bf16[8,2,2,128,128]{4,3,2,1,0:T(8,128)(2,1)S(1)} %get-tuple-element.37) | copy-start | bytes 3145732
  227.5 38.4 %all-to-all-start.1 = ((bf16[8,1,2,2,128,128]{5,4,3,2,1,0:T(8,128)(2,1)}), bf16[8,1,2,2,128,128]{5,4,3,2,1,0:T(8,128)(2,1)}, u32[]{:S(2)}, u32[]{:S(2)}) async-start(bf16[8,1,2,2,128,128]{5,4,3,2,1,0:T(8,128)(2,1)} %bitcast_select_fusion.2), calls=%async_computation.1 | async-start | bytes 2097152 | tf_op jit(solution)/shard_map/all_to_all | solution.py:148
  261.0 18.3 %collective-permute-start = (f32[8,2,128,128]{3,2,0,1:T(8,128)S(1)}, f32[8,2,128,128]{3,2,0,1:T(8,128)}, u32[]{:S(2)}, u32[]{:S(2)}) collective-permute-start(f32[8,2,128,128]{3,2,0,1:T(8,128)S(1)} %pad_maximum_fusion), channel_id=1, source_target_pairs={{0,8},{8,16},{16,24},{24,32},{32,40},{40,48},{48,56},{56,64},{64,7... | collective-permute-start | bytes 3145736 | tf_op jit(solution)/shard_map/ppermute | solution.py:14
  266.0 44.8 %all-to-all-start.2 = ((bf16[8,1,2,2,128,128]{5,4,3,2,1,0:T(8,128)(2,1)}), bf16[8,1,2,2,128,128]{5,4,3,2,1,0:T(8,128)(2,1)S(1)}, u32[]{:S(2)}, u32[]{:S(2)}) async-start(bf16[8,1,2,2,128,128]{5,4,3,2,1,0:T(8,128)(2,1)} %bitcast_select_fusion.1), calls=%async_computation.2 | async-start | bytes 2097152 | tf_op jit(solution)/shard_map/all_to_all | solution.py:148
  275.1 4.2 %copy-start.2 = (f32[2,128,128]{2,1,0:T(8,128)S(1)}, f32[2,128,128]{2,1,0:T(8,128)}, u32[]{:S(2)}) copy-start(f32[2,128,128]{2,1,0:T(8,128)} %param.8) | copy-start | bytes 393220
  305.9 3.8 copy-start.1
  306.9 18.5 %collective-permute-start.1 = (f32[8,2,128,128]{3,2,0,1:T(8,128)}, f32[8,2,128,128]{3,2,0,1:T(8,128)}, u32[]{:S(2)}, u32[]{:S(2)}) collective-permute-start(f32[8,2,128,128]{3,2,0,1:T(8,128)} %pad_maximum_fusion.1), channel_id=1, source_target_pairs={{0,8},{8,16},{16,24},{24,32},{32,40},{40,48},{48,56},{56,64},{64,7... | collective-permute-start | bytes 3145736 | tf_op jit(solution)/shard_map/ppermute | solution.py:14
  310.8 44.9 %all-to-all-start.3 = ((bf16[8,1,2,2,128,128]{5,4,3,2,1,0:T(8,128)(2,1)}), bf16[8,1,2,2,128,128]{5,4,3,2,1,0:T(8,128)(2,1)S(1)}, u32[]{:S(2)}, u32[]{:S(2)}) async-start(bf16[8,1,2,2,128,128]{5,4,3,2,1,0:T(8,128)(2,1)} %bitcast_select_fusion), calls=%async_computation.3 | async-start | bytes 2097152 | tf_op jit(solution)/shard_map/all_to_all | solution.py:148
  352.9 18.4 %collective-permute-start.2 = (f32[8,2,128,128]{3,2,0,1:T(8,128)}, f32[8,2,128,128]{3,2,0,1:T(8,128)S(1)}, u32[]{:S(2)}, u32[]{:S(2)}) collective-permute-start(f32[8,2,128,128]{3,2,0,1:T(8,128)} %pad_maximum_fusion.2), channel_id=1, source_target_pairs={{0,8},{8,16},{16,24},{24,32},{32,40},{40,48},{48,56},{56,64},{64,7... | collective-permute-start | bytes 3145736 | tf_op jit(solution)/shard_map/ppermute | solution.py:14
where the time goes:
time: 404 us; the launch traced here: 398 us
  local copies, waits for them, and re-layouts  118 us (29%)
  matrix products  99.2 us (25%)
  blocking collectives  98.6 us (24%)
  starting transfers between devices  33.7 us (8%)
  waiting for transfers between devices  25.3 us (6%)
  other arithmetic  21 us (5%)
    gather x96, local copies, waits for them, and re-layouts  101 us
    dot_general x96, matrix products, plane_dot(): jnp.dot(flat, table, precision=lax.Precision.HIGHEST, preferred_element_t...  99.2 us
    all_gather x4, blocking collectives, per_device(): lax.all_gather(listing[None], 'tile', axis=0, tiled=True)  83.4 us
    all_to_all x4, starting transfers between devices, per_device(): lax.all_to_all(outgoing(got_lists, got_counts), 'tile', split_axis=0, con...  28 us
    ppermute x3, waiting for transfers between devices, from_behind(): lax.ppermute(value, axis, [(source, source + steps) for source in range(l...  25.3 us
    all_gather x1, blocking collectives, per_device(): lax.all_gather(count[None], 'tile', axis=0, tiled=True)  15.2 us
    unnamed x23, local copies, waits for them, and re-layouts  8.72 us
  transfers between devices with their start and end apart: 7, of which 3 were waited for; matrix products, arithmetic and copies ran while one was open for 44% of the time, Pallas kernels for 0%

commit v1 on v0

--- a/solution.py
+++ b/solution.py
@@ -6,6 +6,11 @@
 
 STEPS = 4
 fresnel_rate = 0.3
+
+
+def gather_by_exchange(shard, axis, dim):
+    copies = jnp.concatenate([shard] * lax.axis_size(axis), axis=dim)
+    return lax.all_to_all(copies, axis, dim, dim, tiled=True)
 
 
 def from_behind(value, axis, steps):
@@ -142,7 +147,7 @@
         else:
             wavefield = wavefield * live
         got_lists, got_counts = (
-            lax.all_gather(listing[None], "tile", axis=0, tiled=True),
+            gather_by_exchange(listing[None], "tile", 0),
             lax.all_gather(count[None], "tile", axis=0, tiled=True),
         )
         received = lax.all_to_all(

time: 404 us -> 347 us (0.86)
  blocking collectives: 98.6 us -> 12.6 us
  starting transfers between devices: 33.7 us -> 56.5 us
  waiting for transfers between devices: 25.3 us -> 34 us
    all_gather x4 -> x0, blocking collectives: 83.4 us -> none  [per_device(): lax.all_gather(listing[None], 'tile', axis=0, tiled=True)]
    all_to_all x0 -> x4, starting transfers between devices: none -> 23 us  [gather_by_exchange(): return lax.all_to_all(copies, axis, dim, dim, tiled=True)]
    all_to_all x0 -> x4, waiting for transfers between devices: none -> 19.1 us  [gather_by_exchange(): return lax.all_to_all(copies, axis, dim, dim, tiled=True)]
    ppermute x3, waiting for transfers between devices: 25.3 us -> 14.9 us  [from_behind(): lax.ppermute(value, axis, [(source, source + steps) for source in range(l...]
    gather x96, local copies, waits for them, and re-layouts: 101 us -> 96.6 us
    unnamed x23 -> x17, local copies, waits for them, and re-layouts: 8.72 us -> 7.89 us
  transfers between devices with their start and end apart: 7 -> 11, of which waited for: 3 -> 4; matrix products, arithmetic and copies ran while one was open for 44% -> 52% of each run, Pallas kernels for 0% -> 0%
where the time goes in v1:
time: 347 us; the launch traced here: 341 us
  local copies, waits for them, and re-layouts  116 us (33%)
  matrix products  99.2 us (29%)
  starting transfers between devices  56.5 us (16%)
  waiting for transfers between devices  34 us (10%)
  other arithmetic  20.3 us (6%)
  blocking collectives  12.6 us (4%)
    dot_general x96, matrix products, plane_dot(): jnp.dot(flat, table, precision=lax.Precision.HIGHEST, preferred_element_t...  99.2 us
    gather x96, local copies, waits for them, and re-layouts  96.6 us
    all_to_all x4, starting transfers between devices, per_device(): lax.all_to_all(outgoing(got_lists, got_counts), 'tile', split_axis=0, con...  26.7 us
    all_to_all x4, starting transfers between devices, gather_by_exchange(): return lax.all_to_all(copies, axis, dim, dim, tiled=True)  23 us
    all_to_all x4, waiting for transfers between devices, gather_by_exchange(): return lax.all_to_all(copies, axis, dim, dim, tiled=True)  19.1 us
    ppermute x3, waiting for transfers between devices, from_behind(): lax.ppermute(value, axis, [(source, source + steps) for source in range(l...  14.9 us
    all_gather x1, blocking collectives, per_device(): lax.all_gather(count[None], 'tile', axis=0, tiled=True)  12.6 us
    unnamed x17, local copies, waits for them, and re-layouts  7.89 us
  transfers between devices with their start and end apart: 11, of which 4 were waited for; matrix products, arithmetic and copies ran while one was open for 52% of the time, Pallas kernels for 0%

profile of v1, /device:TPU:38, one launch (start us, length us, event | category | flops | bytes accessed | tf_op | source)
XLA Modules:
  0.0 340.6 jit_solution(9757497156792930265)
XLA Ops:
  1.8 8.6 %all-to-all-start.2 = ((s32[8,3,8]{2,1,0:T(4,128)}), s32[8,3,8]{2,1,0:T(4,128)S(1)}, u32[]{:S(2)}, u32[]{:S(2)}) async-start(s32[8,3,8]{2,1,0:T(4,128)} %concatenate.26), calls=%async_computation.2 | async-start | bytes 32768 | tf_op jit(solution)/shard_map/all_to_all | solution.py:13
  21.7 12.6 %all-reduce.4 = (s32[8]{0:T(128)S(1)}, s32[8]{0:T(128)S(1)}, s32[8]{0:T(128)S(1)}, s32[8]{0:T(128)S(1)}) all-reduce(s32[8]{0:T(128)S(1)} %bitcast_dynamic-update-slice_fusion.4, s32[8]{0:T(128)S(1)} %bitcast_dynamic-update-slice_fusion.5, s32[8]{0:T(128)S(1)} %bitcast_dynamic-update-slice_fusion.6, ...), channel_id=5, replica_groups=mesh['depth'=32,'tile'=8] {'tile'}, use_global_device_ids=true, to_apply=%add.3 | all-reduce | flops 32 | bytes 256 | tf_op jit(solution)/shard_map/all_gather | solution.py:151
  39.4 5.1 %all-to-all-start.4 = ((s32[8,3,8]{2,1,0:T(4,128)}), s32[8,3,8]{2,1,0:T(4,128)S(1)}, u32[]{:S(2)}, u32[]{:S(2)}) async-start(s32[8,3,8]{2,1,0:T(4,128)} %concatenate.28), calls=%async_computation.4 | async-start | bytes 32768 | tf_op jit(solution)/shard_map/all_to_all | solution.py:13
  44.5 6.4 %all-to-all-done.4 = s32[8,3,8]{2,1,0:T(4,128)S(1)} async-done(((s32[8,3,8]{2,1,0:T(4,128)}), s32[8,3,8]{2,1,0:T(4,128)S(1)}, u32[]{:S(2)}, u32[]{:S(2)}) %all-to-all-start.4) | async-done | bytes 800 | tf_op jit(solution)/shard_map/all_to_all | solution.py:13
  51.4 4.7 %all-to-all-start = ((s32[8,3,8]{2,1,0:T(4,128)}), s32[8,3,8]{2,1,0:T(4,128)S(1)}, u32[]{:S(2)}, u32[]{:S(2)}) async-start(s32[8,3,8]{2,1,0:T(4,128)} %concatenate.24), calls=%async_computation | async-start | bytes 32768 | tf_op jit(solution)/shard_map/all_to_all | solution.py:13
  56.1 6.4 %all-to-all-done = s32[8,3,8]{2,1,0:T(4,128)S(1)} async-done(((s32[8,3,8]{2,1,0:T(4,128)}), s32[8,3,8]{2,1,0:T(4,128)S(1)}, u32[]{:S(2)}, u32[]{:S(2)}) %all-to-all-start) | async-done | bytes 800 | tf_op jit(solution)/shard_map/all_to_all | solution.py:13
  63.1 4.7 %all-to-all-start.6 = ((s32[8,3,8]{2,1,0:T(4,128)}), s32[8,3,8]{2,1,0:T(4,128)S(1)}, u32[]{:S(2)}, u32[]{:S(2)}) async-start(s32[8,3,8]{2,1,0:T(4,128)} %concatenate.30), calls=%async_computation.6 | async-start | bytes 32768 | tf_op jit(solution)/shard_map/all_to_all | solution.py:13
  67.8 6.4 %all-to-all-done.6 = s32[8,3,8]{2,1,0:T(4,128)S(1)} async-done(((s32[8,3,8]{2,1,0:T(4,128)}), s32[8,3,8]{2,1,0:T(4,128)S(1)}, u32[]{:S(2)}, u32[]{:S(2)}) %all-to-all-start.6) | async-done | bytes 800 | tf_op jit(solution)/shard_map/all_to_all | solution.py:13
  75.7 24.7 %while.4 = (s32[]{:T(128)}, bf16[2,2,384,384]{3,2,1,0:T(8,128)(2,1)}, s32[8,4]{0,1:T(4,128)S(1)}, bf16[8,2,2,128,128]{4,3,2,1,0:T(8,128)(2,1)S(1)}, s32[]{:T(128)}) while((s32[]{:T(128)}, bf16[2,2,384,384]{3,2,1,0:T(8,128)(2,1)}, s32[8,4]{0,1:T(4,128)S(1)}, bf16[8,2,2,128,128]{4,3,2,1,0:T(8,128)(2,1)S(1)}, s32[]{:T(128)}) %tuple.106), condition=%wide.while_cond, body=%wide.while_body.sunk | while | flops 2 | bytes 262269 | solution.py:98
  79.5 2.4 bitcast_dynamic-update-slice_fusion.12
  82.6 2.4 bitcast_dynamic-update-slice_fusion.12
  88.8 2.4 bitcast_dynamic-update-slice_fusion.12
  91.9 2.4 bitcast_dynamic-update-slice_fusion.12
  95.0 2.4 bitcast_dynamic-update-slice_fusion.12
  98.0 2.4 bitcast_dynamic-update-slice_fusion.12
  101.6 4.9 %all-to-all-start.1 = ((bf16[8,1,2,2,128,128]{5,4,3,2,1,0:T(8,128)(2,1)}), bf16[8,1,2,2,128,128]{5,4,3,2,1,0:T(8,128)(2,1)S(1)}, u32[]{:S(2)}, u32[]{:S(2)}) async-start(bf16[8,1,2,2,128,128]{5,4,3,2,1,0:T(8,128)(2,1)} %bitcast_select_fusion.3), calls=%async_computation.1 | async-start | bytes 2097152 | tf_op jit(solution)/shard_map/all_to_all | solution.py:153
  106.7 24.6 %while.5 = (s32[]{:T(128)}, bf16[2,2,384,384]{3,2,1,0:T(8,128)(2,1)}, s32[8,4]{0,1:T(4,128)S(1)}, bf16[8,2,2,128,128]{4,3,2,1,0:T(8,128)(2,1)S(1)}, s32[]{:T(128)}) while((s32[]{:T(128)}, bf16[2,2,384,384]{3,2,1,0:T(8,128)(2,1)}, s32[8,4]{0,1:T(4,128)S(1)}, bf16[8,2,2,128,128]{4,3,2,1,0:T(8,128)(2,1)S(1)}, s32[]{:T(128)}) %tuple.118), condition=%wide.while_cond.1, body=%wide.while_body.1.sunk | while | flops 2 | bytes 262269 | solution.py:98
  132.5 7.4 %all-to-all-start.3 = ((bf16[8,1,2,2,128,128]{5,4,3,2,1,0:T(8,128)(2,1)}), bf16[8,1,2,2,128,128]{5,4,3,2,1,0:T(8,128)(2,1)S(1)}, u32[]{:S(2)}, u32[]{:S(2)}) async-start(bf16[8,1,2,2,128,128]{5,4,3,2,1,0:T(8,128)(2,1)} %bitcast_select_fusion.2), calls=%async_computation.3 | async-start | bytes 2097152 | tf_op jit(solution)/shard_map/all_to_all | solution.py:153
  170.3 23.7 %while.6 = (s32[]{:T(128)}, bf16[2,2,384,384]{3,2,1,0:T(8,128)(2,1)}, s32[8,4]{0,1:T(4,128)S(1)}, bf16[8,2,2,128,128]{4,3,2,1,0:T(8,128)(2,1)S(1)}, s32[]{:T(128)}) while((s32[]{:T(128)}, bf16[2,2,384,384]{3,2,1,0:T(8,128)(2,1)}, s32[8,4]{0,1:T(4,128)S(1)}, bf16[8,2,2,128,128]{4,3,2,1,0:T(8,128)(2,1)S(1)}, s32[]{:T(128)}) %tuple.119), condition=%wide.while_cond.2, body=%wide.while_body.2.sunk | while | flops 2 | bytes 262269 | solution.py:98
  195.2 7.2 %all-to-all-start.5 = ((bf16[8,1,2,2,128,128]{5,4,3,2,1,0:T(8,128)(2,1)}), bf16[8,1,2,2,128,128]{5,4,3,2,1,0:T(8,128)(2,1)S(1)}, u32[]{:S(2)}, u32[]{:S(2)}) async-start(bf16[8,1,2,2,128,128]{5,4,3,2,1,0:T(8,128)(2,1)} %bitcast_select_fusion.1), calls=%async_computation.5 | async-start | bytes 2097152 | tf_op jit(solution)/shard_map/all_to_all | solution.py:153
  231.6 3.0 collective-permute-start.1
  234.9 24.0 %while.7 = (s32[]{:T(128)}, bf16[2,2,384,384]{3,2,1,0:T(8,128)(2,1)}, s32[8,4]{0,1:T(4,128)S(1)}, bf16[8,2,2,128,128]{4,3,2,1,0:T(8,128)(2,1)S(1)}, s32[]{:T(128)}) while((s32[]{:T(128)}, bf16[2,2,384,384]{3,2,1,0:T(8,128)(2,1)}, s32[8,4]{0,1:T(4,128)S(1)}, bf16[8,2,2,128,128]{4,3,2,1,0:T(8,128)(2,1)S(1)}, s32[]{:T(128)}) %tuple.120), condition=%wide.while_cond.3, body=%wide.while_body.3.sunk | while | flops 2 | bytes 262269 | solution.py:98
  260.0 7.2 %all-to-all-start.7 = ((bf16[8,1,2,2,128,128]{5,4,3,2,1,0:T(8,128)(2,1)}), bf16[8,1,2,2,128,128]{5,4,3,2,1,0:T(8,128)(2,1)S(1)}, u32[]{:S(2)}, u32[]{:S(2)}) async-start(bf16[8,1,2,2,128,128]{5,4,3,2,1,0:T(8,128)(2,1)} %bitcast_select_fusion), calls=%async_computation.7 | async-start | bytes 2097152 | tf_op jit(solution)/shard_map/all_to_all | solution.py:153
  298.2 14.9 %collective-permute-done.2 = f32[8,2,128,128]{3,2,0,1:T(8,128)} collective-permute-done((f32[8,2,128,128]{3,2,0,1:T(8,128)S(1)}, f32[8,2,128,128]{3,2,0,1:T(8,128)}, u32[]{:S(2)}, u32[]{:S(2)}) %collective-permute-start.2) | collective-permute-done | bytes 1048608 | tf_op jit(solution)/shard_map/ppermute | solution.py:19
  (287 shorter events, 224.9 us)
Async XLA Ops:
  1.8 36.9 %all-to-all-start.2 = ((s32[8,3,8]{2,1,0:T(4,128)}), s32[8,3,8]{2,1,0:T(4,128)S(1)}, u32[]{:S(2)}, u32[]{:S(2)}) async-start(s32[8,3,8]{2,1,0:T(4,128)} %concatenate.26), calls=%async_computation.2 | async-start | bytes 32768 | tf_op jit(solution)/shard_map/all_to_all | solution.py:13
  39.4 11.5 %all-to-all-start.4 = ((s32[8,3,8]{2,1,0:T(4,128)}), s32[8,3,8]{2,1,0:T(4,128)S(1)}, u32[]{:S(2)}, u32[]{:S(2)}) async-start(s32[8,3,8]{2,1,0:T(4,128)} %concatenate.28), calls=%async_computation.4 | async-start | bytes 32768 | tf_op jit(solution)/shard_map/all_to_all | solution.py:13
  51.4 11.0 %all-to-all-start = ((s32[8,3,8]{2,1,0:T(4,128)}), s32[8,3,8]{2,1,0:T(4,128)S(1)}, u32[]{:S(2)}, u32[]{:S(2)}) async-start(s32[8,3,8]{2,1,0:T(4,128)} %concatenate.24), calls=%async_computation | async-start | bytes 32768 | tf_op jit(solution)/shard_map/all_to_all | solution.py:13
  63.1 11.0 %all-to-all-start.6 = ((s32[8,3,8]{2,1,0:T(4,128)}), s32[8,3,8]{2,1,0:T(4,128)S(1)}, u32[]{:S(2)}, u32[]{:S(2)}) async-start(s32[8,3,8]{2,1,0:T(4,128)} %concatenate.30), calls=%async_computation.6 | async-start | bytes 32768 | tf_op jit(solution)/shard_map/all_to_all | solution.py:13
  101.6 30.9 %all-to-all-start.1 = ((bf16[8,1,2,2,128,128]{5,4,3,2,1,0:T(8,128)(2,1)}), bf16[8,1,2,2,128,128]{5,4,3,2,1,0:T(8,128)(2,1)S(1)}, u32[]{:S(2)}, u32[]{:S(2)}) async-start(bf16[8,1,2,2,128,128]{5,4,3,2,1,0:T(8,128)(2,1)} %bitcast_select_fusion.3), calls=%async_computation.1 | async-start | bytes 2097152 | tf_op jit(solution)/shard_map/all_to_all | solution.py:153
  132.5 7.4 %copy-start = (bf16[8,1,2,2,128,128]{5,4,3,2,1,0:T(8,128)(2,1)}, bf16[8,1,2,2,128,128]{5,4,3,2,1,0:T(8,128)(2,1)S(1)}, u32[]{:S(2)}) copy-start(bf16[8,1,2,2,128,128]{5,4,3,2,1,0:T(8,128)(2,1)S(1)} %all-to-all-done.1) | copy-start | bytes 3145732
  132.5 62.7 %all-to-all-start.3 = ((bf16[8,1,2,2,128,128]{5,4,3,2,1,0:T(8,128)(2,1)}), bf16[8,1,2,2,128,128]{5,4,3,2,1,0:T(8,128)(2,1)S(1)}, u32[]{:S(2)}, u32[]{:S(2)}) async-start(bf16[8,1,2,2,128,128]{5,4,3,2,1,0:T(8,128)(2,1)} %bitcast_select_fusion.2), calls=%async_computation.3 | async-start | bytes 2097152 | tf_op jit(solution)/shard_map/all_to_all | solution.py:153
  168.2 35.2 %collective-permute-start = (f32[8,2,128,128]{3,2,0,1:T(8,128)}, f32[8,2,128,128]{3,2,0,1:T(8,128)}, u32[]{:S(2)}, u32[]{:S(2)}) collective-permute-start(f32[8,2,128,128]{3,2,0,1:T(8,128)} %pad_maximum_fusion), channel_id=1, source_target_pairs={{0,8},{8,16},{16,24},{24,32},{32,40},{40,48},{48,56},{56,64},{64,7... | collective-permute-start | bytes 3145736 | tf_op jit(solution)/shard_map/ppermute | solution.py:19
  195.2 64.8 %all-to-all-start.5 = ((bf16[8,1,2,2,128,128]{5,4,3,2,1,0:T(8,128)(2,1)}), bf16[8,1,2,2,128,128]{5,4,3,2,1,0:T(8,128)(2,1)S(1)}, u32[]{:S(2)}, u32[]{:S(2)}) async-start(bf16[8,1,2,2,128,128]{5,4,3,2,1,0:T(8,128)(2,1)} %bitcast_select_fusion.1), calls=%async_computation.5 | async-start | bytes 2097152 | tf_op jit(solution)/shard_map/all_to_all | solution.py:153
  203.2 0.9 copy-start.1
  231.6 36.6 %collective-permute-start.1 = (f32[8,2,128,128]{3,2,0,1:T(8,128)}, f32[8,2,128,128]{3,2,0,1:T(8,128)}, u32[]{:S(2)}, u32[]{:S(2)}) collective-permute-start(f32[8,2,128,128]{3,2,0,1:T(8,128)} %pad_maximum_fusion.1), channel_id=1, source_target_pairs={{0,8},{8,16},{16,24},{24,32},{32,40},{40,48},{48,56},{56,64},{64,7... | collective-permute-start | bytes 3145736 | tf_op jit(solution)/shard_map/ppermute | solution.py:19
  260.0 37.2 %all-to-all-start.7 = ((bf16[8,1,2,2,128,128]{5,4,3,2,1,0:T(8,128)(2,1)}), bf16[8,1,2,2,128,128]{5,4,3,2,1,0:T(8,128)(2,1)S(1)}, u32[]{:S(2)}, u32[]{:S(2)}) async-start(bf16[8,1,2,2,128,128]{5,4,3,2,1,0:T(8,128)(2,1)} %bitcast_select_fusion), calls=%async_computation.7 | async-start | bytes 2097152 | tf_op jit(solution)/shard_map/all_to_all | solution.py:153
  294.8 18.3 %collective-permute-start.2 = (f32[8,2,128,128]{3,2,0,1:T(8,128)S(1)}, f32[8,2,128,128]{3,2,0,1:T(8,128)}, u32[]{:S(2)}, u32[]{:S(2)}) collective-permute-start(f32[8,2,128,128]{3,2,0,1:T(8,128)S(1)} %pad_maximum_fusion.2), channel_id=1, source_target_pairs={{0,8},{8,16},{16,24},{24,32},{32,40},{40,48},{48,56},{56,64},{64,7... | collective-permute-start | bytes 3145736 | tf_op jit(solution)/shard_map/ppermute | solution.py:19
